TPU v7x, 256 devices: a whole 4x4x8 slice. The times are simulated.
256 devices in a mesh: dp: 2 (over core), ctx: 16 (over y, x), tp: 8 (over z).
Axes of the slice: x: 4, y: 4, z: 8, core: 2. Of those that a mesh axis runs over, the one named last changes fastest.
Arguments:
- queries: bfloat16 [2, 8192, 8192], P('dp', 'ctx', 'tp'), may hold values from -120 to 120
- keys: bfloat16 [2, 8192, 8192], P('dp', 'ctx', 'tp'), may hold values from -0.5 to 0.5
- values: bfloat16 [2, 8192, 8192], P('dp', 'ctx', 'tp'), may hold values from -180 to 180
- gate: bfloat16 [2, 8192, 8192], P('dp', 'ctx', 'tp'), may hold values from -8 to 8
- cotangent: bfloat16 [2, 8192, 8192], P('dp', 'ctx', 'tp'), may hold values from -6 to 6
- gain: float32 [8192], P('tp'), may hold values from 0.1 to 1.9
- slopes: float32 [64], P('tp'), may hold values from 1.2207031e-06 to 0.06
Outputs:
- query_gradient: bfloat16 [2, 8192, 8192], P('dp', 'ctx', 'tp')
- key_gradient: bfloat16 [2, 8192, 8192], P('dp', 'ctx', 'tp')
- grad_value: bfloat16 [2, 8192, 8192], P('dp', 'ctx', 'tp')
- grad_gate: bfloat16 [2, 8192, 8192], P('dp', 'ctx', 'tp')
- grad_gain: float32 [8192], P('tp')
All inputs are finite; a program needn't handle non-finite values.
Results may differ from a plain program's by a relative error of at most 0.0062.
Values sent between devices are 32-bit elements; how exact they have to be, the bound alone decides.
A program may use at most 128 MiB of HBM per device.

v0:
```python
import jax
import jax.numpy as jnp
from jax import lax
from jax.sharding import PartitionSpec as P

HD = 128
BLOCK = 512
FEATURES = 8192


EPSILON = 1e-05


def tables(slopes):
    offsets = jnp.arange(BLOCK).astype(jnp.float32)
    distance = offsets[:, None] - offsets[None, :]
    decays = slopes[:, None, None]
    within_block = jnp.where(
        distance[None] >= 0.0, jnp.exp(-decays * jnp.maximum(distance, 0.0)[None]), 0.0
    )
    after = jnp.exp(-slopes[:, None] * (offsets[None, :] + 1.0))
    before = jnp.exp(-slopes[:, None] * (BLOCK - 1.0 - offsets[None, :]))
    whole = jnp.exp(-slopes * BLOCK)
    return (within_block, after, before, whole)


def per_device(queries, keys, values, gate, cotangent, gain, slopes):
    head_count = slopes.shape[0]
    length = queries.shape[1]
    number_blocks = length // BLOCK
    block_shape = (number_blocks, BLOCK, head_count, HD)
    query_blocks = queries.reshape(block_shape)
    key_blocks = keys.reshape(block_shape)
    value_blocks = values.reshape(block_shape)
    within_block, after, before, whole = tables(slopes)
    leading_factor = after.T[None, :, :, None]
    trailing_factor = before.T[None, :, :, None]
    fading = whole[:, None, None]
    device_span = BLOCK * number_blocks
    position = lax.axis_index("ctx")
    empty = jnp.zeros((head_count, HD, HD), jnp.float32)
    powers = jnp.exp(
        -slopes[None, :] * (BLOCK * jnp.arange(number_blocks).astype(jnp.float32))[:, None]
    )
    masked_scores = (
        jnp.einsum("nlhd,nmhd->nhlm", query_blocks, key_blocks, preferred_element_type=jnp.float32)
        * within_block[None]
    ).astype(jnp.bfloat16)
    keys_scaled = (key_blocks * trailing_factor).astype(jnp.bfloat16)
    updates = jnp.einsum(
        "nlhd,nlhe->nhde", keys_scaled, value_blocks, preferred_element_type=jnp.float32
    )
    running = empty
    block_number = 0
    earlier_list = [running]
    running = fading * running + updates[block_number]
    pieces = lax.all_gather(running[None], "ctx", axis=0, tiled=True)
    indices = jnp.arange(pieces.shape[0])
    distance = position - 1 - indices
    factor = jnp.where(
        distance[:, None] >= 0,
        jnp.exp(
            -slopes[None, :] * device_span * jnp.maximum(distance, 0)[:, None].astype(jnp.float32)
        ),
        0.0,
    )
    incoming = jnp.sum(factor[:, :, None, None] * pieces, axis=0)
    memory_state = (powers[:, :, None, None] * incoming[None] + jnp.stack(earlier_list)).astype(
        jnp.bfloat16
    )
    attended = jnp.einsum(
        "nhlm,nmhe->nlhe", masked_scores, value_blocks, preferred_element_type=jnp.float32
    )
    attended = (
        attended
        + jnp.einsum(
            "nlhd,nhde->nlhe", query_blocks, memory_state, preferred_element_type=jnp.float32
        )
        * leading_factor
    )
    flattened = attended.reshape(length, head_count * HD)
    gated = jax.nn.sigmoid(gate[0].astype(jnp.float32))
    upstream = cotangent[0].astype(jnp.float32)
    grad_normed = upstream * gated
    scaled = grad_normed * gain
    totals = lax.psum(
        (jnp.sum(flattened * flattened, axis=1), jnp.sum(scaled * flattened, axis=1)), "tp"
    )
    radius = lax.rsqrt(totals[0] / FEATURES + EPSILON)[:, None]
    grad_gate = (upstream * flattened * radius * gain * gated * (1.0 - gated)).astype(jnp.bfloat16)
    grad_gain = lax.psum(jnp.sum(grad_normed * flattened * radius, axis=0), ("dp", "ctx"))
    grad_attended = (
        (radius * scaled - radius**3 * flattened * totals[1][:, None] / FEATURES)
        .astype(jnp.bfloat16)
        .reshape(block_shape)
    )
    masked_scores_gradient = (
        jnp.einsum(
            "nlhe,nmhe->nhlm", grad_attended, value_blocks, preferred_element_type=jnp.float32
        )
        * within_block[None]
    ).astype(jnp.bfloat16)
    queries_scaled = (query_blocks * leading_factor).astype(jnp.bfloat16)
    returns = jnp.einsum(
        "nlhd,nlhe->nhde", queries_scaled, grad_attended, preferred_element_type=jnp.float32
    )
    running_back = empty
    later_list = [empty] * number_blocks
    for block_number in reversed(range(number_blocks)):
        later_list[block_number] = running_back
        running_back = fading * running_back + returns[block_number]
    pieces = lax.all_gather(running_back[None], "ctx", axis=0, tiled=True)
    indices = jnp.arange(pieces.shape[0])
    distance = indices - position - 1
    factor = jnp.where(
        distance[:, None] >= 0,
        jnp.exp(
            -slopes[None, :] * device_span * jnp.maximum(distance, 0)[:, None].astype(jnp.float32)
        ),
        0.0,
    )
    outgoing = jnp.sum(factor[:, :, None, None] * pieces, axis=0)
    recalled_output = (
        powers[::-1][:, :, None, None] * outgoing[None] + jnp.stack(later_list)
    ).astype(jnp.bfloat16)
    query_gradient = jnp.einsum(
        "nhlm,nmhd->nlhd", masked_scores_gradient, key_blocks, preferred_element_type=jnp.float32
    )
    query_gradient = (
        query_gradient
        + jnp.einsum(
            "nlhe,nhde->nlhd", grad_attended, memory_state, preferred_element_type=jnp.float32
        )
        * leading_factor
    )
    key_gradient = jnp.einsum(
        "nhlm,nlhd->nmhd", masked_scores_gradient, query_blocks, preferred_element_type=jnp.float32
    )
    key_gradient = (
        key_gradient
        + jnp.einsum(
            "nlhe,nhde->nlhd", value_blocks, recalled_output, preferred_element_type=jnp.float32
        )
        * trailing_factor
    )
    grad_value = jnp.einsum(
        "nhlm,nlhe->nmhe", masked_scores, grad_attended, preferred_element_type=jnp.float32
    )
    grad_value = (
        grad_value
        + jnp.einsum(
            "nlhd,nhde->nlhe", key_blocks, recalled_output, preferred_element_type=jnp.float32
        )
        * trailing_factor
    )
    out_shape = (1, length, head_count * HD)
    return (
        query_gradient.astype(jnp.bfloat16).reshape(out_shape),
        key_gradient.astype(jnp.bfloat16).reshape(out_shape),
        grad_value.astype(jnp.bfloat16).reshape(out_shape),
        grad_gate[None],
        grad_gain,
    )


def solution(mesh):
    return jax.shard_map(
        per_device,
        mesh=mesh,
        in_specs=(
            P("dp", "ctx", "tp"),
            P("dp", "ctx", "tp"),
            P("dp", "ctx", "tp"),
            P("dp", "ctx", "tp"),
            P("dp", "ctx", "tp"),
            P("tp"),
            P("tp"),
        ),
        out_specs=(
            P("dp", "ctx", "tp"),
            P("dp", "ctx", "tp"),
            P("dp", "ctx", "tp"),
            P("dp", "ctx", "tp"),
            P("tp"),
        ),
        check_vma=False,
    )
```

profile of v0, /device:TPU:2, one launch (start us, length us, event | category | flops | bytes accessed | tf_op | source)
XLA Modules:
  0.0 246.0 jit_solution(10281232872326610267)
XLA Ops:
  7.2 0.0 all-gather.5.cloned.1.call-start
  7.2 0.7 multiply_exponential_fusion.2
  7.9 1.5 copy.62
  9.4 0.0 copy-start.2
  9.4 0.7 copy.37
  10.1 0.0 copy-start.13
  10.1 1.9 copy.63
  12.0 0.0 copy-start.4
  12.0 0.1 multiply_exponential_fusion.1
  12.1 1.3 convolution_add_fusion.1
  13.3 0.0 copy-done.13
  13.3 0.0 all-gather.5.cloned.1.call-update
  13.4 0.0 all-gather.7.cloned.1.call-start
  13.4 1.5 copy.61
  14.9 0.0 copy-start.6
  15.0 0.1 exponential_select_fusion.1
  15.1 0.2 subtract_compare_fusion
  15.3 0.1 subtract_maximum_fusion
  15.5 0.0 copy-start.15
  15.5 0.0 copy-done.2
  15.5 2.9 %multiply_convert_fusion.1 = bf16[8,512,512]{2,1,0:T(8,128)(2,1)S(1)} fusion(f32[512,512]{1,0:T(8,128)S(1)} %subtract_maximum_fusion, f32[8]{0:T(128)S(1)} %get-tuple-element.26, pred[512,512]{1,0:T(8,128)(4,1)S(1)} %subtract_compare_fusion, bf16[512,8,128]{0,2,1:T(8,128)(2,1)S(1)} %bitcast.92, bf16[512,8,128]{2,1,0:T(8,128)(2,1)S(1)} %bitcast.86), kind=kOutput, calls=%fused_computation.3 | convolution fusion | flops 545259520 | bytes 7602208 | tf_op jit(solution)/shard_map/nlhd,nmhd->nhlm/dot_general | solution.py:46
  18.3 0.0 copy-done.4
  18.4 0.0 copy-done.15
  18.4 0.0 copy-start
  18.4 2.0 copy-done
  20.3 2.8 %fusion.17 = f32[8,512,128]{1,2,0:T(8,128)} fusion(bf16[8,512,512]{2,1,0:T(8,128)(2,1)S(1)} %multiply_convert_fusion.1, bf16[512,8,128]{2,1,0:T(8,128)(2,1)S(1)} %bitcast.89), kind=kOutput, calls=%fused_computation.39 | convolution fusion | flops 536870912 | bytes 7340032 | tf_op jit(solution)/shard_map/nhlm,nmhe->nlhe/dot_general | solution.py:71
  23.2 69.1 %all-gather.5.cloned.1.call-done = f32[128,128,128]{2,1,0:T(8,128)} async-done(((f32[8,128,128]{2,1,0:T(8,128)}), f32[128,128,128]{2,1,0:T(8,128)}) %all-gather.5.cloned.1.call-update) | async-done | bytes 8388624 | tf_op jit(solution)/shard_map/all_gather | solution.py:57
  92.2 4.2 %multiply_reduce_fusion.1 = f32[8,128,128]{2,1,0:T(8,128)S(1)} fusion(f32[16,8,128,128]{3,2,1,0:T(8,128)} %bitcast.96, f32[16,8]{1,0:T(8,128)S(1)} %get-tuple-element.22), kind=kLoop, calls=%fused_computation.2 | loop fusion | flops 4063232 | bytes 8913408 | tf_op jit(solution)/shard_map/reduce_sum | solution.py:67
  96.4 0.0 copy-start.11
  96.5 0.0 copy-done.6
  96.5 0.0 copy-done.10
  96.5 0.7 multiply_reduce_fusion.4
  97.2 0.1 copy-done.11
  97.2 17.4 %psum.21 = f32[512]{0:T(512)S(1)} all-reduce(f32[512]{0:T(512)S(1)} %get-tuple-element.29), channel_id=1, replica_groups=mesh['dp'=2,'ctx'=16,'tp'=8] {'tp'}, use_global_device_ids=true, to_apply=%region_2.3 | all-reduce | flops 512 | bytes 4096 | tf_op jit(solution)/shard_map/psum | solution.py:86
  114.7 1.8 copy.52
  116.6 0.0 copy-done.17
  116.6 0.0 copy-done.18
  116.6 4.6 %fusion.4 = (bf16[1,512,1024]{2,1,0:T(8,128)(2,1)}, f32[1,512,1024]{2,1,0:T(8,128)}) fusion(f32[1,512,1024]{2,1,0:T(8,128)} %copy.52, bf16[1,512,1024]{2,1,0:T(8,128)(2,1)S(1)} %copy-done.17, f32[1024]{0:T(1024)S(1)} %copy-done.18, f32[512]{0:T(512)S(1)} %get-tuple-element.20, bf16[1,512,1024]{2,1,0:T(8,128)(2,1)} %param.10), kind=kLoop, calls=%fused_computation.11 | loop fusion | flops 6815744 | bytes 7346176 | tf_op jit(solution)/shard_map/convert_element_type | solution.py:90
  121.2 2.9 %copy.41 = f32[1,512,1024]{1,2,0:T(8,128)} copy(f32[1,512,1024]{2,1,0:T(8,128)} %get-tuple-element.18) | data formatting | bytes 4194304 | tf_op jit(solution)/shard_map/mul | solution.py:84
  124.1 2.1 multiply_reduce_fusion.2
  126.2 15.2 %psum.22 = f32[512]{0:T(512)S(1)} all-reduce(f32[512]{0:T(512)S(1)} %get-tuple-element.16), channel_id=1, replica_groups=mesh['dp'=2,'ctx'=16,'tp'=8] {'tp'}, use_global_device_ids=true, to_apply=%region_4.5 | all-reduce | flops 512 | bytes 4096 | tf_op jit(solution)/shard_map/psum | solution.py:86
  141.4 2.2 fusion.12
  143.6 0.0 copy-done.7
  143.6 0.0 copy-start.5
  143.6 0.0 copy-start.16
  143.6 1.3 convolution_add_fusion
  144.9 0.0 all-gather.7.cloned.1.call-update
  144.9 0.4 copy-done.16
  145.4 2.8 %multiply_convert_fusion = bf16[8,512,512]{2,1,0:T(8,128)(2,1)S(1)} fusion(f32[512,512]{1,0:T(8,128)S(1)} %copy-done.16, f32[8]{0:T(128)S(1)} %get-tuple-element.26, pred[512,512]{1,0:T(8,128)(4,1)S(1)} %subtract_compare_fusion, bf16[512,8,128]{0,2,1:T(8,128)(2,1)S(1)} %fusion.12, bf16[512,8,128]{2,1,0:T(8,128)(2,1)S(1)} %bitcast.90), kind=kOutput, calls=%fused_computation.1 | convolution fusion | flops 545259520 | bytes 7602208 | tf_op jit(solution)/shard_map/nlhe,nmhe->nhlm/dot_general | solution.py:98
  148.2 1.5 fusion.27
  149.7 0.4 copy-done.1
  150.1 0.0 copy-done.12
  150.1 1.5 fusion.10
  151.6 2.3 copy.53
  153.9 64.9 %psum.23 = f32[1024]{0:T(1024)} all-reduce(f32[1024]{0:T(1024)S(1)} %bitcast.105), channel_id=1, replica_groups=mesh['dp'=2,'ctx'=16,'tp'=8] {'dp','ctx'}, use_global_device_ids=true, to_apply=%region_7.8 | all-reduce | flops 1024 | bytes 8192 | tf_op jit(solution)/shard_map/psum | solution.py:91
  218.8 4.2 %fusion.28 = f32[8,128,512]{2,1,0:T(8,128)} fusion(bf16[512,8,128]{0,2,1:T(8,128)(2,1)S(1)} %fusion.12, bf16[8,512,512]{2,1,0:T(8,128)(2,1)} %copy-done), kind=kOutput, calls=%fused_computation.66 | convolution fusion | flops 536870912 | bytes 7340032 | tf_op jit(solution)/shard_map/nhlm,nlhe->nmhe/dot_general | solution.py:146
  223.0 4.1 %multiply_reduce_fusion = f32[8,128,128]{2,1,0:T(8,128)S(1)} fusion(f32[16,8,128,128]{3,2,1,0:T(8,128)} %bitcast.97, f32[16,8]{1,0:T(8,128)S(1)} %get-tuple-element.21), kind=kLoop, calls=%fused_computation | loop fusion | flops 4063232 | bytes 8913408 | tf_op jit(solution)/shard_map/reduce_sum | solution.py:122
  227.1 0.5 fusion.19
  227.6 0.7 copy-done.3
  228.3 0.7 copy-done.9
  229.0 1.6 fusion.6
  230.7 2.4 copy.55
  233.0 3.9 %fusion.8 = bf16[1,512,8,128]{1,3,2,0:T(8,128)(2,1)} fusion(f32[8,128,512]{2,1,0:T(8,128)S(1)} %fusion.19, bf16[512,8,128]{0,2,1:T(8,128)(2,1)S(1)} %bitcast.95, bf16[8,512,512]{2,1,0:T(8,128)(2,1)} %copy-done.1, f32[512,8]{0,1:T(8,128)S(1)} %get-tuple-element.27), kind=kOutput, calls=%fused_computation.17 | convolution fusion | flops 538443776 | bytes 8404992 | tf_op jit(solution)/shard_map/nhlm,nlhd->nmhd/dot_general | solution.py:136
  236.9 2.3 copy.54
  (19 shorter events, 0.1 us)
Async XLA Ops:
  7.2 85.1 %all-gather.5.cloned.1.call-start = ((), (), s32[]{:S(2)}) async-start(), calls=%async_computation | async-start | bytes 8912896 | tf_op jit(solution)/shard_map/all_gather | solution.py:57
  9.4 6.1 %copy-start.2 = (bf16[64,8,8,128]{3,2,1,0:T(8,128)(2,1)}, bf16[64,8,8,128]{3,2,1,0:T(8,128)(2,1)S(1)}, u32[]{:S(2)}) copy-start(bf16[64,8,8,128]{3,2,1,0:T(8,128)(2,1)S(1)} %copy.62) | copy-start | bytes 3145732
  10.1 3.3 %copy-start.13 = (bf16[512,8,128]{0,2,1:T(8,128)(2,1)}, bf16[512,8,128]{0,2,1:T(8,128)(2,1)S(1)}, u32[]{:S(2)}) copy-start(bf16[512,8,128]{0,2,1:T(8,128)(2,1)S(1)} %copy.37) | copy-start | bytes 3145732
  12.0 6.4 %copy-start.4 = (bf16[64,8,8,128]{3,2,1,0:T(8,128)(2,1)}, bf16[64,8,8,128]{3,2,1,0:T(8,128)(2,1)S(1)}, u32[]{:S(2)}) copy-start(bf16[64,8,8,128]{3,2,1,0:T(8,128)(2,1)S(1)} %copy.63) | copy-start | bytes 3145732
  13.4 209.7 %all-gather.7.cloned.1.call-start = ((), (), s32[]{:S(2)}) async-start(), calls=%async_computation.1 | async-start | bytes 8912896 | tf_op jit(solution)/shard_map/all_gather | solution.py:112
  14.9 81.5 %copy-start.6 = (bf16[1,512,1024]{1,2,0:T(8,128)(2,1)}, bf16[1,512,1024]{1,2,0:T(8,128)(2,1)S(1)}, u32[]{:S(2)}) copy-start(bf16[1,512,1024]{1,2,0:T(8,128)(2,1)S(1)} %copy.61) | copy-start | bytes 3145732
  15.5 2.9 %copy-start.15 = (f32[512,512]{1,0:T(8,128)}, f32[512,512]{1,0:T(8,128)S(1)}, u32[]{:S(2)}) copy-start(f32[512,512]{1,0:T(8,128)S(1)} %subtract_maximum_fusion) | copy-start | bytes 3145732
  18.4 2.0 copy-start
  92.2 4.2 %copy-start.10 = (f32[8,512,128]{1,2,0:T(8,128)S(1)}, f32[8,512,128]{1,2,0:T(8,128)}, u32[]{:S(2)}) copy-start(f32[8,512,128]{1,2,0:T(8,128)} %fusion.17) | copy-start | bytes 6291460
  96.4 0.8 copy-start.11
  114.7 1.9 copy-start.17
  114.7 1.9 copy-start.18
  141.4 2.2 copy-start.7
  143.6 1.3 copy-start.5
  143.6 1.7 copy-start.16
  145.3 2.8 %copy-start.14 = (bf16[512,8,128]{0,2,1:T(8,128)(2,1)S(1)}, bf16[512,8,128]{0,2,1:T(8,128)(2,1)}, u32[]{:S(2)}) copy-start(bf16[512,8,128]{0,2,1:T(8,128)(2,1)} %copy-done.13) | copy-start | bytes 3145732
  148.2 1.9 copy-start.1
  148.2 1.9 copy-start.12
  227.1 1.2 copy-start.3
  227.1 1.9 copy-start.9
  230.7 2.4 copy-start.8
Sparse Core Ops, SparseCore 0:
  13.5 78.6 all-gather.4
  145.1 73.4 all-gather.6
where the time goes:
time: 250 us; the launch traced here: 246 us
  blocking collectives  97.6 us (39%)
  waiting for transfers between devices  69.1 us (28%)
  matrix products  24.9 us (10%)
  local copies, waits for them, and re-layouts  21.5 us (9%)
  other arithmetic  18.4 us (7%)
  between operations  14.4 us (6%)
    all_gather x1, waiting for transfers between devices, per_device(): pieces = lax.all_gather(running[None], 'ctx', axis=0, tiled=True)  69.1 us
    psum x1, blocking collectives, per_device(): lax.psum(jnp.sum(grad_normed * flattened * radius, axis=0), ('dp', 'ctx'))  64.9 us
    psum x2, blocking collectives, per_device(): lax.psum((jnp.sum(flattened * flattened, axis=1), jnp.sum(scaled * flatte...  32.6 us
    unnamed x43, local copies, waits for them, and re-layouts  14.6 us
  transfers between devices with their start and end apart: 2, of which 1 were waited for; matrix products, arithmetic and copies ran while one was open for 8% of the time, Pallas kernels for 0%

commit v1 on v0

v1 whole, which is shorter than its diff:
```python
import functools

import jax
import jax.numpy as jnp
from jax import lax
from jax.experimental import pallas as pl
from jax.experimental.pallas import tpu as pltpu
from jax.sharding import PartitionSpec as P

HD = 128
BLOCK = 512
FEATURES = 8192
HEADS_HERE = 8
HALF = BLOCK // 2
CTX_X = 4
CTX_Y = 4
CTX = CTX_X * CTX_Y
TP = 8
CHUNKS = 4
PER = HEADS_HERE // CHUNKS
PART = HD // CTX
ROWS = PER * PART
EPSILON = 1e-05
MESH = pl.DeviceIdType.MESH

F32 = jnp.float32
BF16 = jnp.bfloat16

OFFSETS = sorted(
    [(dx, dy) for dx in range(CTX_X) for dy in range(CTX_Y) if (dx, dy) != (0, 0)],
    key=lambda o: -(min(o[0], CTX_X - o[0]) + min(o[1], CTX_Y - o[1])),
)
TP_OFFSETS = (4, 3, 5, 2, 6, 1, 7)

NN = (((1,), (0,)), ((), ()))
NT = (((1,), (1,)), ((), ()))
TN = (((0,), (0,)), ((), ()))


def dot(a, b, dims):
    return lax.dot_general(a, b, dims, preferred_element_type=F32)


def kernel(
    slopes, q_in, k_in, v_in, g_in, c_in, gain_ref,
    dq_out, dk_out, dv_out, dg_out, gain_out,
    q, k, v, g, c, dq, dk, dv, dg,
    after, before, masked, w_near, w_far, att, nrm, omg, qst, ga, mem, gm, dki, dvi,
    sq, cr, rcol, ccol,
    u, r1, s2, r2, zsend, zrecv, gsend, gpart, gboth, grecv,
    load_sem, out_sem, send1, recv1, send2, recv2, zs_sem, zr_sem, g_sem,
):
    me = lax.axis_index("ctx")
    me_x, me_y = lax.rem(me, CTX_X), lax.div(me, CTX_X)
    my_tp = lax.axis_index("tp")
    my_dp = lax.axis_index("dp")
    ctx_peers = [
        lax.rem(me_y + dy, CTX_Y) * CTX_X + lax.rem(me_x + dx, CTX_X) for dx, dy in OFFSETS
    ]
    tp_peers = [lax.rem(my_tp + o, TP) for o in TP_OFFSETS]
    partner = 1 - my_dp

    def load(n, src, dst, h):
        return pltpu.make_async_copy(
            src.at[0, :, pl.ds(pl.multiple_of(h * HD, HD), HD)], dst.at[h], load_sem.at[n, h]
        )

    def store(n, src, dst, h):
        return pltpu.make_async_copy(
            src.at[h], dst.at[0, :, pl.ds(pl.multiple_of(h * HD, HD), HD)], out_sem.at[n, h]
        )

    def load_kv(h, _):
        load(1, k_in, k, h).start()
        load(2, v_in, v, h).start()
        return 0

    def load_rest(h, _):
        load(0, q_in, q, h).start()
        load(3, g_in, g, h).start()
        load(4, c_in, c, h).start()
        return 0

    lax.fori_loop(0, HEADS_HERE, load_kv, 0)
    barrier = pltpu.get_barrier_semaphore()
    for p in ctx_peers:
        pl.semaphore_signal(barrier, inc=1, device_id={"ctx": p}, device_id_type=MESH)
    for p in tp_peers:
        pl.semaphore_signal(barrier, inc=1, device_id={"tp": p}, device_id_type=MESH)
    pl.semaphore_signal(barrier, inc=1, device_id={"dp": partner}, device_id_type=MESH)
    lax.fori_loop(0, HEADS_HERE, load_rest, 0)

    position = lax.broadcasted_iota(jnp.int32, (BLOCK, HD), 0).astype(F32)

    def exchange(src, dst, send, recv, n, p):
        return pltpu.make_async_remote_copy(
            src_ref=src.at[n, p],
            dst_ref=dst.at[n, me],
            send_sem=send.at[n],
            recv_sem=recv.at[n],
            device_id={"ctx": p},
            device_id_type=MESH,
        )

    def send_all(src, dst, send, recv, n):
        for p in ctx_peers:
            exchange(src, dst, send, recv, n, p).start()
        dst[n, me] = src[n, me]

    def waiter(src, dst, send, recv, n):
        return pltpu.make_async_remote_copy(
            src_ref=src.at[n, pl.ds(0, CTX - 1)],
            dst_ref=dst.at[n, pl.ds(0, CTX - 1)],
            send_sem=send.at[n],
            recv_sem=recv.at[n],
            device_id={"ctx": ctx_peers[0]},
            device_id_type=MESH,
        )

    def scan(d, n, reverse):
        waiter(u.at[d], r1.at[d], send1.at[d], recv1.at[d], n).wait_recv()
        fade = jnp.concatenate(
            [
                jnp.exp(jnp.full((PART, HD), -slopes[n * PER + i] * BLOCK, F32))
                for i in range(PER)
            ],
            axis=0,
        )
        total = jnp.zeros((ROWS, HD), F32)
        for b in reversed(range(CTX)) if reverse else range(CTX):
            s2[d, n, b] = total
            total = fade * total + r1[d, n, b]
        send_all(s2.at[d], r2.at[d], send2.at[d], recv2.at[d], n)

    def state(d, n, i):
        return r2[d, n, :, i * PART : (i + 1) * PART, :].reshape(HD, HD).astype(BF16)

    def put(d, n, i, value):
        u[d, n, :, i * PART : (i + 1) * PART, :] = value.reshape(CTX, PART, HD)

    def summary(n):
        for i in range(PER):
            h = n * PER + i
            load(1, k_in, k, h).wait()
            load(2, v_in, v, h).wait()
            weight = jnp.exp(-slopes[h] * (BLOCK - 1.0 - position))
            before[h] = weight
            scaled_keys = (k[h].astype(F32) * weight).astype(BF16)
            put(0, n, i, dot(scaled_keys, v[h], TN))

    def first(n, _):
        summary(n)
        send_all(u.at[0], r1.at[0], send1.at[0], recv1.at[0], n)
        return 0

    summary(0)
    pl.semaphore_wait(barrier, CTX - 1 + TP - 1 + 1)
    send_all(u.at[0], r1.at[0], send1.at[0], recv1.at[0], 0)
    lax.fori_loop(1, CHUNKS, first, 0)

    distance = (
        lax.broadcasted_iota(jnp.int32, (HALF, HALF), 0)
        - lax.broadcasted_iota(jnp.int32, (HALF, HALF), 1)
    ).astype(F32)

    def inside(h, _):
        load(0, q_in, q, h).wait()
        load(3, g_in, g, h).wait()
        load(4, c_in, c, h).wait()
        rate = slopes[h]
        near = jnp.where(distance >= 0.0, jnp.exp(-rate * jnp.maximum(distance, 0.0)), 0.0)
        far = jnp.exp(-rate * (distance + HALF))
        w_near[h] = near
        w_far[h] = far
        top, bottom = q[h, :HALF], q[h, HALF:]
        k_top, k_bottom = k[h, :HALF], k[h, HALF:]
        masked[h, 0] = (dot(top, k_top, NT) * near).astype(BF16)
        masked[h, 1] = (dot(bottom, k_top, NT) * far).astype(BF16)
        masked[h, 2] = (dot(bottom, k_bottom, NT) * near).astype(BF16)
        att[h, :HALF] = dot(masked[h, 0], v[h, :HALF], NN)
        att[h, HALF:] = dot(masked[h, 1], v[h, :HALF], NN) + dot(masked[h, 2], v[h, HALF:], NN)
        weight = jnp.exp(-rate * (position + 1.0))
        after[h] = weight
        qst[h] = (q[h].astype(F32) * weight).astype(BF16).T
        gated = 1.0 / (1.0 + jnp.exp(-g[h].astype(F32)))
        nrm[h] = c[h].astype(F32) * gated
        omg[h] = 1.0 - gated
        return 0

    def scan_forward(n, _):
        scan(0, n, False)
        return 0

    lax.fori_loop(0, HEADS_HERE // 2, inside, 0)
    lax.fori_loop(0, CHUNKS, scan_forward, 0)
    lax.fori_loop(HEADS_HERE // 2, HEADS_HERE, inside, 0)

    sq[...] = jnp.zeros_like(sq)
    cr[...] = jnp.zeros_like(cr)

    def attend(n, _):
        waiter(s2.at[0], r2.at[0], send2.at[0], recv2.at[0], n).wait_recv()
        for i in range(PER):
            h = n * PER + i
            memory = state(0, n, i)
            mem[h] = memory
            attended = att[h] + after[h] * dot(q[h], memory, NN)
            att[h] = attended
            sq[...] += attended * attended
            cr[...] += nrm[h] * gain_ref[pl.ds(h, 1), :] * attended
        return 0

    lax.fori_loop(0, CHUNKS, attend, 0)
    rows = [
        jnp.sum(ref[t * HD : (t + 1) * HD, :].T, axis=0, keepdims=True)
        for ref in (sq, cr)
        for t in range(BLOCK // HD)
    ]
    zsend[...] = jnp.concatenate(rows, axis=0)

    def tp_copy(i):
        return pltpu.make_async_remote_copy(
            src_ref=zsend,
            dst_ref=zrecv.at[my_tp],
            send_sem=zs_sem.at[i],
            recv_sem=zr_sem.at[i],
            device_id={"tp": tp_peers[i]},
            device_id_type=MESH,
        )

    for i in range(TP - 1):
        tp_copy(i).start()
    zrecv[my_tp] = zsend[...]
    for i in range(TP - 1):
        tp_copy(i).wait_recv()
    totals = zrecv[0]
    for i in range(1, TP):
        totals = totals + zrecv[i]
    radius = lax.rsqrt(totals[:4] / FEATURES + EPSILON)
    cross = radius * radius * radius * totals[4:] / FEATURES
    for t in range(BLOCK // HD):
        rows_here = pl.ds(t * HD, HD)
        rcol[rows_here, :] = jnp.broadcast_to(radius[t : t + 1], (HD, HD)).T
        ccol[rows_here, :] = jnp.broadcast_to(cross[t : t + 1], (HD, HD)).T

    def second(n, _):
        for i in range(PER):
            h = n * PER + i
            scaled = nrm[h] * gain_ref[pl.ds(h, 1), :]
            gradient = (rcol[...] * scaled - ccol[...] * att[h]).astype(BF16)
            ga[h] = gradient
            put(1, n, i, dot(qst[h], gradient, NN))
        send_all(u.at[1], r1.at[1], send1.at[1], recv1.at[1], n)
        return 0

    lax.fori_loop(0, CHUNKS, second, 0)

    def gate(h, _):
        common = nrm[h] * att[h] * rcol[...]
        gsend[pl.ds(h, 1), :] = jnp.sum(common, axis=0, keepdims=True)
        dg[h] = (common * gain_ref[pl.ds(h, 1), :] * omg[h]).astype(BF16)
        store(3, dg, dg_out, h).start()
        return 0

    lax.fori_loop(0, HEADS_HERE, gate, 0)
    pair = pltpu.make_async_remote_copy(
        src_ref=gsend,
        dst_ref=gpart,
        send_sem=g_sem.at[0],
        recv_sem=g_sem.at[1],
        device_id={"dp": partner},
        device_id_type=MESH,
    )
    pair.start()

    def backward(h, _):
        gradient = ga[h]
        g_top, g_bottom = ga[h, :HALF], ga[h, HALF:]
        v_top, v_bottom = v[h, :HALF], v[h, HALF:]
        near, far = w_near[h], w_far[h]
        m0 = (dot(g_top, v_top, NT) * near).astype(BF16)
        m1 = (dot(g_bottom, v_top, NT) * far).astype(BF16)
        m2 = (dot(g_bottom, v_bottom, NT) * near).astype(BF16)
        gm[0] = m0
        gm[1] = m1
        gm[2] = m2
        k_top, k_bottom = k[h, :HALF], k[h, HALF:]
        carried = after[h] * dot(gradient, mem[h], NT)
        dq[h, :HALF] = (dot(gm[0], k_top, NN) + carried[:HALF]).astype(BF16)
        dq[h, HALF:] = (
            dot(gm[1], k_top, NN) + dot(gm[2], k_bottom, NN) + carried[HALF:]
        ).astype(BF16)
        store(0, dq, dq_out, h).start()
        dki[h, :HALF] = dot(gm[0], q[h, :HALF], TN) + dot(gm[1], q[h, HALF:], TN)
        dki[h, HALF:] = dot(gm[2], q[h, HALF:], TN)
        dvi[h, :HALF] = dot(masked[h, 0], g_top, TN) + dot(masked[h, 1], g_bottom, TN)
        dvi[h, HALF:] = dot(masked[h, 2], g_bottom, TN)
        return 0

    def scan_backward(n, _):
        scan(1, n, True)
        return 0

    lax.fori_loop(0, HEADS_HERE // 4, backward, 0)
    pair.wait_recv()
    gboth[...] = gsend[...] + gpart[...]
    lax.fori_loop(0, CHUNKS, scan_backward, 0)

    def gain_copy(p):
        return pltpu.make_async_remote_copy(
            src_ref=gboth,
            dst_ref=grecv.at[me],
            send_sem=g_sem.at[2],
            recv_sem=g_sem.at[3],
            device_id={"ctx": p},
            device_id_type=MESH,
        )

    for p in ctx_peers:
        gain_copy(p).start()
    grecv[me] = gboth[...]
    lax.fori_loop(HEADS_HERE // 4, HEADS_HERE, backward, 0)

    def sent(n, _):
        waiter(u.at[0], r1.at[0], send1.at[0], recv1.at[0], n).wait_send()
        waiter(s2.at[0], r2.at[0], send2.at[0], recv2.at[0], n).wait_send()
        waiter(u.at[1], r1.at[1], send1.at[1], recv1.at[1], n).wait_send()
        return 0

    lax.fori_loop(0, CHUNKS, sent, 0)
    for i in range(TP - 1):
        tp_copy(i).wait_send()
    pair.wait_send()

    def finish(n, _):
        waiter(s2.at[1], r2.at[1], send2.at[1], recv2.at[1], n).wait_recv()
        for i in range(PER):
            h = n * PER + i
            recalled = state(1, n, i)
            dk[h] = (dki[h] + before[h] * dot(v[h], recalled, NT)).astype(BF16)
            store(1, dk, dk_out, h).start()
            dv[h] = (dvi[h] + before[h] * dot(k[h], recalled, NN)).astype(BF16)
            store(2, dv, dv_out, h).start()
        return 0

    lax.fori_loop(0, CHUNKS, finish, 0)

    gain_all = pltpu.make_async_remote_copy(
        src_ref=grecv.at[pl.ds(0, CTX - 1)],
        dst_ref=grecv.at[pl.ds(0, CTX - 1)],
        send_sem=g_sem.at[2],
        recv_sem=g_sem.at[3],
        device_id={"ctx": ctx_peers[0]},
        device_id_type=MESH,
    )
    gain_all.wait_recv()
    gain_all.wait_send()
    total = grecv[0]
    for i in range(1, CTX):
        total = total + grecv[i]
    gain_out[...] = total

    def drain(n, _):
        waiter(s2.at[1], r2.at[1], send2.at[1], recv2.at[1], n).wait_send()
        return 0

    def stored(h, _):
        store(0, dq, dq_out, h).wait()
        store(1, dk, dk_out, h).wait()
        store(2, dv, dv_out, h).wait()
        store(3, dg, dg_out, h).wait()
        return 0

    lax.fori_loop(0, CHUNKS, drain, 0)
    lax.fori_loop(0, HEADS_HERE, stored, 0)


def per_device(queries, keys, values, gate, cotangent, gain, slopes):
    whole = jax.ShapeDtypeStruct((1, BLOCK, HEADS_HERE * HD), BF16)
    heads16 = pltpu.VMEM((HEADS_HERE, BLOCK, HD), BF16)
    heads32 = pltpu.VMEM((HEADS_HERE, BLOCK, HD), F32)
    column = pltpu.VMEM((BLOCK, HD), F32)
    travel = pltpu.VMEM((2, CHUNKS, CTX, ROWS, HD), F32)
    tile = pltpu.VMEM((HEADS_HERE, HD), F32)
    dma = pltpu.SemaphoreType.DMA
    scratch = (
        [heads16] * 9
        + [
            heads32,
            heads32,
            pltpu.VMEM((HEADS_HERE, 3, HALF, HALF), BF16),
            pltpu.VMEM((HEADS_HERE, HALF, HALF), F32),
            pltpu.VMEM((HEADS_HERE, HALF, HALF), F32),
            heads32,
            heads32,
            heads32,
            pltpu.VMEM((HEADS_HERE, HD, BLOCK), BF16),
            heads16,
            pltpu.VMEM((HEADS_HERE, HD, HD), BF16),
            pltpu.VMEM((3, HALF, HALF), BF16),
            heads32,
            heads32,
        ]
        + [column] * 4
        + [travel] * 4
        + [
            tile,
            pltpu.VMEM((TP, 8, HD), F32),
            tile,
            tile,
            tile,
            pltpu.VMEM((CTX, HEADS_HERE, HD), F32),
            dma((5, HEADS_HERE)),
            dma((4, HEADS_HERE)),
        ]
        + [dma((2, CHUNKS))] * 4
        + [dma((TP - 1,)), dma((TP - 1,)), dma((4,))]
    )
    anywhere = pl.BlockSpec(memory_space=pl.ANY)
    in_vmem = pl.BlockSpec(memory_space=pltpu.VMEM)
    flops = HEADS_HERE * BLOCK * HD * 2 * (6 * BLOCK * 3 // 4 + 6 * HD)
    dq, dk, dv, dg, total = pl.pallas_call(
        kernel,
        out_shape=(whole, whole, whole, whole, jax.ShapeDtypeStruct((HEADS_HERE, HD), F32)),
        in_specs=[pl.BlockSpec(memory_space=pltpu.SMEM)] + [anywhere] * 5 + [in_vmem],
        out_specs=(anywhere, anywhere, anywhere, anywhere, in_vmem),
        scratch_shapes=scratch,
        compiler_params=pltpu.CompilerParams(
            collective_id=0, has_side_effects=True, vmem_limit_bytes=56 << 20
        ),
        cost_estimate=pl.CostEstimate(
            flops=flops, bytes_accessed=9 << 20, transcendentals=HEADS_HERE * BLOCK * BLOCK
        ),
        name="lightning_backward",
    )(slopes, queries, keys, values, gate, cotangent, gain.reshape(HEADS_HERE, HD))
    return dq, dk, dv, dg, total.reshape(HEADS_HERE * HD)


def solution(mesh):
    wide = P("dp", "ctx", "tp")
    return jax.shard_map(
        per_device,
        mesh=mesh,
        in_specs=(wide, wide, wide, wide, wide, P("tp"), P("tp")),
        out_specs=(wide, wide, wide, wide, P("tp")),
        check_vma=False,
    )
```

time: 250 us -> 53.6 us (0.21); the launches traced: 246 us -> 53.3 us
  blocking collectives: 97.6 us -> 0 us
  waiting for transfers between devices: 69.1 us -> 0 us
  Pallas kernels: 0 us -> 45.6 us
  matrix products: 24.9 us -> 0 us
  other arithmetic: 18.4 us -> 0 us
  local copies, waits for them, and re-layouts: 21.5 us -> 7.13 us
  between operations: 14.4 us -> 0.66 us
    psum x3 -> x0, blocking collectives: 97.6 us -> none  [the longest x1 64.9 us: per_device(): lax.psum(jnp.sum(grad_normed * flattened * radius, axis=0), ('dp', 'ctx'))]
    all_gather x2 -> x0, waiting for transfers between devices: 69.1 us -> none  [the longest x1 69.1 us: per_device(): pieces = lax.all_gather(running[None], 'ctx', axis=0, tiled=True)]
    pallas_call x0 -> x1, Pallas kernels: none -> 45.6 us  [per_device(): pl.pallas_call(kernel, out_shape=(whole, whole, whole, whole, jax.ShapeDt...]
    dot_general x12 -> x0, matrix products: 24.9 us -> none  [the longest x1 4.23 us: per_device(): jnp.einsum('nhlm,nlhe->nmhe', masked_scores, grad_attended, preferred_ele...]
    reduce_sum x3 -> x0, other arithmetic: 10.4 us -> none  [the longest x1 4.2 us: per_device(): incoming = jnp.sum(factor[:, :, None, None] * pieces, axis=0)]
    unnamed x43 -> x13, local copies, waits for them, and re-layouts: 14.6 us -> 7.13 us
    convert_element_type x3 -> x0, other arithmetic: 4.62 us -> none  [the longest x1 4.61 us: per_device(): (upstream * flattened * radius * gain * gated * (1.0 - gated)).astype(jnp...]
    reshape x2 -> x0, local copies, waits for them, and re-layouts: 3.35 us -> none  [the longest x1 1.85 us: per_device(): flattened = attended.reshape(length, head_count * HD)]
  transfers between devices with their start and end apart: 2 -> 0, of which waited for: 1 -> 0; matrix products, arithmetic and copies ran while one was open for 8% -> 0% of each run, Pallas kernels for 0% -> 0%
where the time goes in v1:
time: 53.6 us; the launch traced here: 53.3 us
  Pallas kernels  45.6 us (85%)
  local copies, waits for them, and re-layouts  7.13 us (13%)
  between operations  0.66 us (1%)
    pallas_call x1, Pallas kernels, per_device(): pl.pallas_call(kernel, out_shape=(whole, whole, whole, whole, jax.ShapeDt...  45.6 us
    unnamed x13, local copies, waits for them, and re-layouts  7.13 us

profile of v1, /device:TPU:2, one launch (start us, length us, event | category | flops | bytes accessed | tf_op | source)
XLA Modules:
  0.0 53.3 jit_solution(16555123934052040529)
XLA Ops:
  0.6 45.6 %lightning_backward.1 = (bf16[1,512,1024]{2,1,0:T(8,128)(2,1)}, bf16[1,512,1024]{2,1,0:T(8,128)(2,1)}, bf16[1,512,1024]{2,1,0:T(8,128)(2,1)}, bf16[1,512,1024]{2,1,0:T(8,128)(2,1)}, f32[8,128]{1,0:T(8,128)}) custom-call(f32[8]{0:T(128)} %slopes.1, bf16[1,512,1024]{2,1,0:T(8,128)(2,1)} %q_in.1, bf16[1,512,1024]{2,1,0:T(8,128)(2,1)} %k_in.1, ...), custom_call_target="tpu_custom_call" | custom-call | flops 3221225472 | bytes 9437184 | tf_op jit(solution)/shard_map/lightning_backward/pallas_call | solution.py:422
  46.2 0.0 copy-start.2
  46.2 2.4 %copy.17 = bf16[1,512,1024]{2,1,0:T(8,128)(2,1)} copy(bf16[1,512,1024]{2,1,0:T(8,128)(2,1)} %get-tuple-element.20) | data formatting | bytes 2097152
  48.6 0.0 copy-done.2
  48.6 0.0 copy-start.1
  48.6 1.0 %copy.18 = bf16[1,512,1024]{2,1,0:T(8,128)(2,1)} copy(bf16[1,512,1024]{2,1,0:T(8,128)(2,1)S(1)} %copy-done.2) | data formatting | bytes 2097152
  49.5 0.6 %copy-done.1 = bf16[1,512,1024]{2,1,0:T(8,128)(2,1)S(1)} copy-done((bf16[1,512,1024]{2,1,0:T(8,128)(2,1)S(1)}, bf16[1,512,1024]{2,1,0:T(8,128)(2,1)}, u32[]{:S(2)}) %copy-start.1) | copy-done | bytes 1048600
  50.2 0.0 copy-start
  50.2 1.0 %copy.19 = bf16[1,512,1024]{2,1,0:T(8,128)(2,1)} copy(bf16[1,512,1024]{2,1,0:T(8,128)(2,1)S(1)} %copy-done.1) | data formatting | bytes 2097152
  51.1 0.6 %copy-done = bf16[1,512,1024]{2,1,0:T(8,128)(2,1)S(1)} copy-done((bf16[1,512,1024]{2,1,0:T(8,128)(2,1)S(1)}, bf16[1,512,1024]{2,1,0:T(8,128)(2,1)}, u32[]{:S(2)}) %copy-start) | copy-done | bytes 1048600
  51.8 0.0 copy-start.3
  51.8 1.0 %copy.20 = bf16[1,512,1024]{2,1,0:T(8,128)(2,1)} copy(bf16[1,512,1024]{2,1,0:T(8,128)(2,1)S(1)} %copy-done) | data formatting | bytes 2097152
  52.8 0.0 copy-done.3
  52.8 0.6 %copy.21 = f32[1024]{0:T(1024)} copy(f32[1024]{0:T(1024)S(1)} %bitcast.2) | data formatting | bytes 8192
Async XLA Ops:
  46.2 2.4 %copy-start.2 = (bf16[1,512,1024]{2,1,0:T(8,128)(2,1)S(1)}, bf16[1,512,1024]{2,1,0:T(8,128)(2,1)}, u32[]{:S(2)}) copy-start(bf16[1,512,1024]{2,1,0:T(8,128)(2,1)} %get-tuple-element.21) | copy-start | bytes 3145732
  48.6 1.6 %copy-start.1 = (bf16[1,512,1024]{2,1,0:T(8,128)(2,1)S(1)}, bf16[1,512,1024]{2,1,0:T(8,128)(2,1)}, u32[]{:S(2)}) copy-start(bf16[1,512,1024]{2,1,0:T(8,128)(2,1)} %get-tuple-element.22) | copy-start | bytes 3145732
  50.2 1.6 %copy-start = (bf16[1,512,1024]{2,1,0:T(8,128)(2,1)S(1)}, bf16[1,512,1024]{2,1,0:T(8,128)(2,1)}, u32[]{:S(2)}) copy-start(bf16[1,512,1024]{2,1,0:T(8,128)(2,1)} %get-tuple-element.23) | copy-start | bytes 3145732
  51.8 1.0 %copy-start.3 = (f32[8,128]{1,0:T(8,128)S(1)}, f32[8,128]{1,0:T(8,128)}, u32[]{:S(2)}) copy-start(f32[8,128]{1,0:T(8,128)} %get-tuple-element.14) | copy-start | bytes 12292

commit v2 on v1

--- a/solution.py
+++ b/solution.py
@@ -19,6 +19,7 @@
 CHUNKS = 4
 PER = HEADS_HERE // CHUNKS
 PART = HD // CTX
+PIECE = 512
 ROWS = PER * PART
 EPSILON = 1e-05
 MESH = pl.DeviceIdType.MESH
@@ -35,6 +36,7 @@
 NN = (((1,), (0,)), ((), ()))
 NT = (((1,), (1,)), ((), ()))
 TN = (((0,), (0,)), ((), ()))
+TT = (((0,), (1,)), ((), ()))
 
 
 def dot(a, b, dims):
@@ -42,13 +44,13 @@
 
 
 def kernel(
-    slopes, q_in, k_in, v_in, g_in, c_in, gain_ref,
-    dq_out, dk_out, dv_out, dg_out, gain_out,
-    q, k, v, g, c, dq, dk, dv, dg,
-    after, before, masked, w_near, w_far, att, nrm, omg, qst, ga, mem, gm, dki, dvi,
-    sq, cr, rcol, ccol,
+    slopes_in, q_in, k_in, v_in, g_in, c_in, gain_in,
+    dq, dk, dv, dg, gain_out,
+    slopes, gain_ref, q, k, v, g, c,
+    after, before, masked, w_near, w_far, att_t, sca_t, nrm, omg, qst, ga_t, ga, mem, gm, dki, dvi,
+    sums, stats, rcol,
     u, r1, s2, r2, zsend, zrecv, gsend, gpart, gboth, grecv,
-    load_sem, out_sem, send1, recv1, send2, recv2, zs_sem, zr_sem, g_sem,
+    small_sem, load_sem, send1, recv1, send2, recv2, zs_sem, zr_sem, g_sem,
 ):
     me = lax.axis_index("ctx")
     me_x, me_y = lax.rem(me, CTX_X), lax.div(me, CTX_X)
@@ -65,11 +67,6 @@
             src.at[0, :, pl.ds(pl.multiple_of(h * HD, HD), HD)], dst.at[h], load_sem.at[n, h]
         )
 
-    def store(n, src, dst, h):
-        return pltpu.make_async_copy(
-            src.at[h], dst.at[0, :, pl.ds(pl.multiple_of(h * HD, HD), HD)], out_sem.at[n, h]
-        )
-
     def load_kv(h, _):
         load(1, k_in, k, h).start()
         load(2, v_in, v, h).start()
@@ -81,16 +78,26 @@
         load(4, c_in, c, h).start()
         return 0
 
-    lax.fori_loop(0, HEADS_HERE, load_kv, 0)
+    def lanes(h):
+        return pl.ds(pl.multiple_of(h * HD, HD), HD)
+
+    slopes_copy = pltpu.make_async_copy(slopes_in, slopes, small_sem.at[0])
+    gain_copy_in = pltpu.make_async_copy(gain_in, gain_ref, small_sem.at[1])
+    slopes_copy.start()
+    lax.fori_loop(0, PER, load_kv, 0)
     barrier = pltpu.get_barrier_semaphore()
     for p in ctx_peers:
         pl.semaphore_signal(barrier, inc=1, device_id={"ctx": p}, device_id_type=MESH)
     for p in tp_peers:
         pl.semaphore_signal(barrier, inc=1, device_id={"tp": p}, device_id_type=MESH)
     pl.semaphore_signal(barrier, inc=1, device_id={"dp": partner}, device_id_type=MESH)
+    lax.fori_loop(PER, HEADS_HERE, load_kv, 0)
+    gain_copy_in.start()
     lax.fori_loop(0, HEADS_HERE, load_rest, 0)
+    slopes_copy.wait()
 
     position = lax.broadcasted_iota(jnp.int32, (BLOCK, HD), 0).astype(F32)
+    along = lax.broadcasted_iota(jnp.int32, (1, BLOCK), 1).astype(F32)
 
     def exchange(src, dst, send, recv, n, p):
         return pltpu.make_async_remote_copy(
@@ -141,11 +148,12 @@
     def summary(n):
         for i in range(PER):
             h = n * PER + i
+            before[h] = jnp.exp(-slopes[h] * (BLOCK - 1.0 - position))
+        for i in range(PER):
+            h = n * PER + i
             load(1, k_in, k, h).wait()
             load(2, v_in, v, h).wait()
-            weight = jnp.exp(-slopes[h] * (BLOCK - 1.0 - position))
-            before[h] = weight
-            scaled_keys = (k[h].astype(F32) * weight).astype(BF16)
+            scaled_keys = (k[h].astype(F32) * before[h]).astype(BF16)
             put(0, n, i, dot(scaled_keys, v[h], TN))
 
     def first(n, _):
@@ -177,13 +185,17 @@
         masked[h, 0] = (dot(top, k_top, NT) * near).astype(BF16)
         masked[h, 1] = (dot(bottom, k_top, NT) * far).astype(BF16)
         masked[h, 2] = (dot(bottom, k_bottom, NT) * near).astype(BF16)
-        att[h, :HALF] = dot(masked[h, 0], v[h, :HALF], NN)
-        att[h, HALF:] = dot(masked[h, 1], v[h, :HALF], NN) + dot(masked[h, 2], v[h, HALF:], NN)
+        att_t[h, :, :HALF] = dot(masked[h, 0], v[h, :HALF], NN).T
+        att_t[h, :, HALF:] = (
+            dot(masked[h, 1], v[h, :HALF], NN) + dot(masked[h, 2], v[h, HALF:], NN)
+        ).T
         weight = jnp.exp(-rate * (position + 1.0))
         after[h] = weight
         qst[h] = (q[h].astype(F32) * weight).astype(BF16).T
         gated = 1.0 / (1.0 + jnp.exp(-g[h].astype(F32)))
-        nrm[h] = c[h].astype(F32) * gated
+        normed = c[h].astype(F32) * gated
+        nrm[h] = normed
+        sca_t[h] = (normed * gain_ref[pl.ds(h, 1), :]).T
         omg[h] = 1.0 - gated
         return 0
 
@@ -191,12 +203,12 @@
         scan(0, n, False)
         return 0
 
+    gain_copy_in.wait()
     lax.fori_loop(0, HEADS_HERE // 2, inside, 0)
     lax.fori_loop(0, CHUNKS, scan_forward, 0)
     lax.fori_loop(HEADS_HERE // 2, HEADS_HERE, inside, 0)
 
-    sq[...] = jnp.zeros_like(sq)
-    cr[...] = jnp.zeros_like(cr)
+    sums[...] = jnp.zeros_like(sums)
 
     def attend(n, _):
         waiter(s2.at[0], r2.at[0], send2.at[0], recv2.at[0], n).wait_recv()
@@ -204,18 +216,18 @@
             h = n * PER + i
             memory = state(0, n, i)
             mem[h] = memory
-            attended = att[h] + after[h] * dot(q[h], memory, NN)
-            att[h] = attended
-            sq[...] += attended * attended
-            cr[...] += nrm[h] * gain_ref[pl.ds(h, 1), :] * attended
+            fade = jnp.exp(-slopes[h] * (along + 1.0))
+            attended = att_t[h] + fade * dot(memory, q[h], TT)
+            att_t[h] = attended
+            sums[0] += jnp.sum((attended * attended).reshape(HD // 8, 8, BLOCK), axis=0)
+            sums[1] += jnp.sum((sca_t[h] * attended).reshape(HD // 8, 8, BLOCK), axis=0)
         return 0
 
     lax.fori_loop(0, CHUNKS, attend, 0)
-    rows = [
-        jnp.sum(ref[t * HD : (t + 1) * HD, :].T, axis=0, keepdims=True)
-        for ref in (sq, cr)
-        for t in range(BLOCK // HD)
-    ]
+    rows = []
+    for n in range(2):
+        row = jnp.sum(sums[n], axis=0, keepdims=True)
+        rows += [row[:, t * HD : (t + 1) * HD] for t in range(BLOCK // HD)]
     zsend[...] = jnp.concatenate(rows, axis=0)
 
     def tp_copy(i):
@@ -238,28 +250,29 @@
         totals = totals + zrecv[i]
     radius = lax.rsqrt(totals[:4] / FEATURES + EPSILON)
     cross = radius * radius * radius * totals[4:] / FEATURES
-    for t in range(BLOCK // HD):
-        rows_here = pl.ds(t * HD, HD)
-        rcol[rows_here, :] = jnp.broadcast_to(radius[t : t + 1], (HD, HD)).T
-        ccol[rows_here, :] = jnp.broadcast_to(cross[t : t + 1], (HD, HD)).T
+    stats[0] = jnp.concatenate([radius[t : t + 1] for t in range(4)], axis=1)
+    stats[1] = jnp.concatenate([cross[t : t + 1] for t in range(4)], axis=1)
 
     def second(n, _):
         for i in range(PER):
             h = n * PER + i
-            scaled = nrm[h] * gain_ref[pl.ds(h, 1), :]
-            gradient = (rcol[...] * scaled - ccol[...] * att[h]).astype(BF16)
-            ga[h] = gradient
-            put(1, n, i, dot(qst[h], gradient, NN))
+            gradient = (stats[0] * sca_t[h] - stats[1] * att_t[h]).astype(BF16)
+            ga_t[h] = gradient
+            put(1, n, i, dot(qst[h], gradient, NT))
         send_all(u.at[1], r1.at[1], send1.at[1], recv1.at[1], n)
         return 0
 
     lax.fori_loop(0, CHUNKS, second, 0)
 
+    for t in range(BLOCK // HD):
+        column = stats[0, :, t * HD : (t + 1) * HD]
+        rcol[t * HD : (t + 1) * HD, :] = jnp.broadcast_to(column, (HD, HD)).T
+
     def gate(h, _):
-        common = nrm[h] * att[h] * rcol[...]
+        ga[h] = ga_t[h].T
+        common = nrm[h] * att_t[h].T * rcol[...]
         gsend[pl.ds(h, 1), :] = jnp.sum(common, axis=0, keepdims=True)
-        dg[h] = (common * gain_ref[pl.ds(h, 1), :] * omg[h]).astype(BF16)
-        store(3, dg, dg_out, h).start()
+        dg[:, lanes(h)] = (common * gain_ref[pl.ds(h, 1), :] * omg[h]).astype(BF16)
         return 0
 
     lax.fori_loop(0, HEADS_HERE, gate, 0)
@@ -286,11 +299,10 @@
         gm[2] = m2
         k_top, k_bottom = k[h, :HALF], k[h, HALF:]
         carried = after[h] * dot(gradient, mem[h], NT)
-        dq[h, :HALF] = (dot(gm[0], k_top, NN) + carried[:HALF]).astype(BF16)
-        dq[h, HALF:] = (
+        dq[:HALF, lanes(h)] = (dot(gm[0], k_top, NN) + carried[:HALF]).astype(BF16)
+        dq[HALF:, lanes(h)] = (
             dot(gm[1], k_top, NN) + dot(gm[2], k_bottom, NN) + carried[HALF:]
         ).astype(BF16)
-        store(0, dq, dq_out, h).start()
         dki[h, :HALF] = dot(gm[0], q[h, :HALF], TN) + dot(gm[1], q[h, HALF:], TN)
         dki[h, HALF:] = dot(gm[2], q[h, HALF:], TN)
         dvi[h, :HALF] = dot(masked[h, 0], g_top, TN) + dot(masked[h, 1], g_bottom, TN)
@@ -337,10 +349,8 @@
         for i in range(PER):
             h = n * PER + i
             recalled = state(1, n, i)
-            dk[h] = (dki[h] + before[h] * dot(v[h], recalled, NT)).astype(BF16)
-            store(1, dk, dk_out, h).start()
-            dv[h] = (dvi[h] + before[h] * dot(k[h], recalled, NN)).astype(BF16)
-            store(2, dv, dv_out, h).start()
+            dk[:, lanes(h)] = (dki[h] + before[h] * dot(v[h], recalled, NT)).astype(BF16)
+            dv[:, lanes(h)] = (dvi[h] + before[h] * dot(k[h], recalled, NN)).astype(BF16)
         return 0
 
     lax.fori_loop(0, CHUNKS, finish, 0)
@@ -364,44 +374,61 @@
         waiter(s2.at[1], r2.at[1], send2.at[1], recv2.at[1], n).wait_send()
         return 0
 
-    def stored(h, _):
-        store(0, dq, dq_out, h).wait()
-        store(1, dk, dk_out, h).wait()
-        store(2, dv, dv_out, h).wait()
-        store(3, dg, dg_out, h).wait()
-        return 0
-
     lax.fori_loop(0, CHUNKS, drain, 0)
-    lax.fori_loop(0, HEADS_HERE, stored, 0)
+
+
+def place(dq_in, dk_in, dv_in, dg_in, gain_in, dq, dk, dv, dg, gain, sem):
+    pairs = ((dq_in, dq), (dk_in, dk), (dv_in, dv), (dg_in, dg))
+    copies = [
+        pltpu.make_async_copy(
+            src.at[pl.ds(i * PIECE, PIECE)], dst.at[0, pl.ds(i * PIECE, PIECE)], sem.at[n, i]
+        )
+        for i in range(BLOCK // PIECE)
+        for n, (src, dst) in enumerate(pairs)
+    ]
+    for copy in copies:
+        copy.start()
+    gain[...] = gain_in[...]
+    for copy in copies:
+        copy.wait()
 
 
 def per_device(queries, keys, values, gate, cotangent, gain, slopes):
     whole = jax.ShapeDtypeStruct((1, BLOCK, HEADS_HERE * HD), BF16)
+    flat = pltpu.VMEM((BLOCK, HEADS_HERE * HD), BF16)
     heads16 = pltpu.VMEM((HEADS_HERE, BLOCK, HD), BF16)
     heads32 = pltpu.VMEM((HEADS_HERE, BLOCK, HD), F32)
-    column = pltpu.VMEM((BLOCK, HD), F32)
+    heads16_t = pltpu.VMEM((HEADS_HERE, HD, BLOCK), BF16)
+    heads32_t = pltpu.VMEM((HEADS_HERE, HD, BLOCK), F32)
     travel = pltpu.VMEM((2, CHUNKS, CTX, ROWS, HD), F32)
     tile = pltpu.VMEM((HEADS_HERE, HD), F32)
     dma = pltpu.SemaphoreType.DMA
     scratch = (
-        [heads16] * 9
+        [pltpu.SMEM((HEADS_HERE,), F32), tile]
+        + [heads16] * 5
         + [
             heads32,
             heads32,
             pltpu.VMEM((HEADS_HERE, 3, HALF, HALF), BF16),
             pltpu.VMEM((HEADS_HERE, HALF, HALF), F32),
             pltpu.VMEM((HEADS_HERE, HALF, HALF), F32),
-            heads32,
-            heads32,
-            heads32,
-            pltpu.VMEM((HEADS_HERE, HD, BLOCK), BF16),
+            heads32_t,
+            heads32_t,
+            heads32,
+            heads32,
+            heads16_t,
+            heads16_t,
             heads16,
             pltpu.VMEM((HEADS_HERE, HD, HD), BF16),
             pltpu.VMEM((3, HALF, HALF), BF16),
             heads32,
             heads32,
         ]
-        + [column] * 4
+        + [
+            pltpu.VMEM((2, 8, BLOCK), F32),
+            pltpu.VMEM((2, 1, BLOCK), F32),
+            pltpu.VMEM((BLOCK, HD), F32),
+        ]
         + [travel] * 4
         + [
             tile,
@@ -410,29 +437,47 @@
             tile,
             tile,
             pltpu.VMEM((CTX, HEADS_HERE, HD), F32),
+            dma((2,)),
             dma((5, HEADS_HERE)),
-            dma((4, HEADS_HERE)),
         ]
         + [dma((2, CHUNKS))] * 4
         + [dma((TP - 1,)), dma((TP - 1,)), dma((4,))]
     )
     anywhere = pl.BlockSpec(memory_space=pl.ANY)
+    in_hbm = pl.BlockSpec(memory_space=pltpu.HBM)
     in_vmem = pl.BlockSpec(memory_space=pltpu.VMEM)
     flops = HEADS_HERE * BLOCK * HD * 2 * (6 * BLOCK * 3 // 4 + 6 * HD)
-    dq, dk, dv, dg, total = pl.pallas_call(
+    whole_inputs = [
+        pltpu.with_memory_space_constraint(x, pltpu.HBM)
+        for x in (
+            slopes, queries, keys, values, gate, cotangent, gain.reshape(HEADS_HERE, HD)
+        )
+    ]
+    results = pl.pallas_call(
         kernel,
-        out_shape=(whole, whole, whole, whole, jax.ShapeDtypeStruct((HEADS_HERE, HD), F32)),
-        in_specs=[pl.BlockSpec(memory_space=pltpu.SMEM)] + [anywhere] * 5 + [in_vmem],
-        out_specs=(anywhere, anywhere, anywhere, anywhere, in_vmem),
+        out_shape=(flat, flat, flat, flat, tile),
+        in_specs=[in_hbm] * 7,
+        out_specs=(in_vmem,) * 5,
         scratch_shapes=scratch,
         compiler_params=pltpu.CompilerParams(
-            collective_id=0, has_side_effects=True, vmem_limit_bytes=56 << 20
+            collective_id=0, has_side_effects=True, vmem_limit_bytes=44 << 20
         ),
         cost_estimate=pl.CostEstimate(
-            flops=flops, bytes_accessed=9 << 20, transcendentals=HEADS_HERE * BLOCK * BLOCK
+            flops=flops, bytes_accessed=5 << 20, transcendentals=HEADS_HERE * BLOCK * BLOCK
         ),
         name="lightning_backward",
-    )(slopes, queries, keys, values, gate, cotangent, gain.reshape(HEADS_HERE, HD))
+    )(*whole_inputs)
+    results = [pltpu.with_memory_space_constraint(x, pltpu.VMEM) for x in results]
+    dq, dk, dv, dg, total = pl.pallas_call(
+        place,
+        out_shape=(whole, whole, whole, whole, jax.ShapeDtypeStruct((HEADS_HERE, HD), F32)),
+        in_specs=[in_vmem] * 5,
+        out_specs=(anywhere,) * 4 + (in_vmem,),
+        scratch_shapes=[dma((4, BLOCK // PIECE))],
+        compiler_params=pltpu.CompilerParams(vmem_limit_bytes=2 << 20),
+        cost_estimate=pl.CostEstimate(flops=0, bytes_accessed=8 << 20, transcendentals=0),
+        name="place_results",
+    )(*results)
     return dq, dk, dv, dg, total.reshape(HEADS_HERE * HD)
 
 

time: 53.6 us -> 46.6 us (0.87)
  local copies, waits for them, and re-layouts: 7.13 us -> 0 us
    unnamed x13 -> x0, local copies, waits for them, and re-layouts: 7.13 us -> none
    pallas_call x1 -> x2, Pallas kernels: 45.6 us -> 45.8 us  [the longest x1 43.2 us: per_device(): pl.pallas_call(kernel, out_shape=(flat, flat, flat, flat, tile), in_specs...]
where the time goes in v2:
time: 46.6 us; the launch traced here: 46.5 us
  Pallas kernels  45.8 us (98%)
  between operations  0.64 us (1%)
    pallas_call x1, Pallas kernels, per_device(): pl.pallas_call(kernel, out_shape=(flat, flat, flat, flat, tile), in_specs...  43.2 us
    pallas_call x1, Pallas kernels, per_device(): pl.pallas_call(place, out_shape=(whole, whole, whole, whole, jax.ShapeDty...  2.63 us

profile of v2, /device:TPU:2, one launch (start us, length us, event | category | flops | bytes accessed | tf_op | source)
XLA Modules:
  0.0 46.5 jit_solution(10741799122846738093)
XLA Ops:
  0.6 43.2 %lightning_backward.1 = (bf16[512,1024]{1,0:T(8,128)(2,1)S(1)}, bf16[512,1024]{1,0:T(8,128)(2,1)S(1)}, bf16[512,1024]{1,0:T(8,128)(2,1)S(1)}, bf16[512,1024]{1,0:T(8,128)(2,1)S(1)}, f32[8,128]{1,0:T(8,128)S(1)}) custom-call(f32[8]{0:T(128)} %slopes_in.1, bf16[1,512,1024]{2,1,0:T(8,128)(2,1)} %q_in.1, bf16[1,512,1024]{2,1,0:T(8,128)(2,1)} %k_in.1, ...), custom_call_target="tpu_custom_call" | custom-call | flops 3221225472 | bytes 5242880 | tf_op jit(solution)/shard_map/lightning_backward/pallas_call | solution.py:456
  43.8 2.6 %place_results.1 = (bf16[1,512,1024]{2,1,0:T(8,128)(2,1)}, bf16[1,512,1024]{2,1,0:T(8,128)(2,1)}, bf16[1,512,1024]{2,1,0:T(8,128)(2,1)}, bf16[1,512,1024]{2,1,0:T(8,128)(2,1)}, f32[8,128]{1,0:T(8,128)}) custom-call(bf16[512,1024]{1,0:T(8,128)(2,1)S(1)} %get-tuple-element.15.dq_in, bf16[512,1024]{1,0:T(8,128)(2,1)S(1)} %get-tuple-element.16.dk_in, ...), custom_call_target="tpu_custom_call" | custom-call | bytes 8388608 | tf_op jit(solution)/shard_map/place_results/pallas_call | solution.py:471

commit v3 on v2

--- a/solution.py
+++ b/solution.py
@@ -36,7 +36,6 @@
 NN = (((1,), (0,)), ((), ()))
 NT = (((1,), (1,)), ((), ()))
 TN = (((0,), (0,)), ((), ()))
-TT = (((0,), (1,)), ((), ()))
 
 
 def dot(a, b, dims):
@@ -47,9 +46,9 @@
     slopes_in, q_in, k_in, v_in, g_in, c_in, gain_in,
     dq, dk, dv, dg, gain_out,
     slopes, gain_ref, q, k, v, g, c,
-    after, before, masked, w_near, w_far, att_t, sca_t, nrm, omg, qst, ga_t, ga, mem, gm, dki, dvi,
+    after, before, masked, w_near, w_far, att_t, sca_t, nrm, omg, qs, q_t, ga_t, ga, mem, gm, dki, dvi,
     sums, stats, rcol,
-    u, r1, s2, r2, zsend, zrecv, gsend, gpart, gboth, grecv,
+    u, r1, s2, r2, zsend, zrecv, gsend, gpart, gsum, grecv,
     small_sem, load_sem, send1, recv1, send2, recv2, zs_sem, zr_sem, g_sem,
 ):
     me = lax.axis_index("ctx")
@@ -81,16 +80,16 @@
     def lanes(h):
         return pl.ds(pl.multiple_of(h * HD, HD), HD)
 
-    slopes_copy = pltpu.make_async_copy(slopes_in, slopes, small_sem.at[0])
-    gain_copy_in = pltpu.make_async_copy(gain_in, gain_ref, small_sem.at[1])
-    slopes_copy.start()
-    lax.fori_loop(0, PER, load_kv, 0)
     barrier = pltpu.get_barrier_semaphore()
     for p in ctx_peers:
         pl.semaphore_signal(barrier, inc=1, device_id={"ctx": p}, device_id_type=MESH)
     for p in tp_peers:
         pl.semaphore_signal(barrier, inc=1, device_id={"tp": p}, device_id_type=MESH)
     pl.semaphore_signal(barrier, inc=1, device_id={"dp": partner}, device_id_type=MESH)
+    slopes_copy = pltpu.make_async_copy(slopes_in, slopes, small_sem.at[0])
+    gain_copy_in = pltpu.make_async_copy(gain_in, gain_ref, small_sem.at[1])
+    slopes_copy.start()
+    lax.fori_loop(0, PER, load_kv, 0)
     lax.fori_loop(PER, HEADS_HERE, load_kv, 0)
     gain_copy_in.start()
     lax.fori_loop(0, HEADS_HERE, load_rest, 0)
@@ -154,7 +153,7 @@
             load(1, k_in, k, h).wait()
             load(2, v_in, v, h).wait()
             scaled_keys = (k[h].astype(F32) * before[h]).astype(BF16)
-            put(0, n, i, dot(scaled_keys, v[h], TN))
+            put(0, n, i, dot(v[h], scaled_keys, TN))
 
     def first(n, _):
         summary(n)
@@ -191,7 +190,8 @@
         ).T
         weight = jnp.exp(-rate * (position + 1.0))
         after[h] = weight
-        qst[h] = (q[h].astype(F32) * weight).astype(BF16).T
+        qs[h] = (q[h].astype(F32) * weight).astype(BF16)
+        q_t[h] = q[h].T
         gated = 1.0 / (1.0 + jnp.exp(-g[h].astype(F32)))
         normed = c[h].astype(F32) * gated
         nrm[h] = normed
@@ -217,7 +217,7 @@
             memory = state(0, n, i)
             mem[h] = memory
             fade = jnp.exp(-slopes[h] * (along + 1.0))
-            attended = att_t[h] + fade * dot(memory, q[h], TT)
+            attended = att_t[h] + fade * dot(memory, q_t[h], NN)
             att_t[h] = attended
             sums[0] += jnp.sum((attended * attended).reshape(HD // 8, 8, BLOCK), axis=0)
             sums[1] += jnp.sum((sca_t[h] * attended).reshape(HD // 8, 8, BLOCK), axis=0)
@@ -258,7 +258,7 @@
             h = n * PER + i
             gradient = (stats[0] * sca_t[h] - stats[1] * att_t[h]).astype(BF16)
             ga_t[h] = gradient
-            put(1, n, i, dot(qst[h], gradient, NT))
+            put(1, n, i, dot(gradient, qs[h], NN))
         send_all(u.at[1], r1.at[1], send1.at[1], recv1.at[1], n)
         return 0
 
@@ -298,7 +298,7 @@
         gm[1] = m1
         gm[2] = m2
         k_top, k_bottom = k[h, :HALF], k[h, HALF:]
-        carried = after[h] * dot(gradient, mem[h], NT)
+        carried = after[h] * dot(gradient, mem[h], NN)
         dq[:HALF, lanes(h)] = (dot(gm[0], k_top, NN) + carried[:HALF]).astype(BF16)
         dq[HALF:, lanes(h)] = (
             dot(gm[1], k_top, NN) + dot(gm[2], k_bottom, NN) + carried[HALF:]
@@ -313,25 +313,42 @@
         scan(1, n, True)
         return 0
 
-    lax.fori_loop(0, HEADS_HERE // 4, backward, 0)
+    lax.fori_loop(0, 3, backward, 0)
     pair.wait_recv()
-    gboth[...] = gsend[...] + gpart[...]
+    gsum[0] = gsend[...] + gpart[...]
+
+    def gain_copy(stage, o):
+        place = lax.rem((me_x, me_y)[stage] + o, 4)
+        return pltpu.make_async_remote_copy(
+            src_ref=gsum.at[stage],
+            dst_ref=grecv.at[stage, (me_x, me_y)[stage]],
+            send_sem=g_sem.at[2 + 2 * stage],
+            recv_sem=g_sem.at[3 + 2 * stage],
+            device_id={"ctx": (me_y * CTX_X + place, place * CTX_X + me_x)[stage]},
+            device_id_type=MESH,
+        )
+
+    def gain_start(stage):
+        for o in (2, 1, 3):
+            gain_copy(stage, o).start()
+        grecv[stage, (me_x, me_y)[stage]] = gsum[stage]
+
+    def gain_all(stage):
+        return pltpu.make_async_remote_copy(
+            src_ref=grecv.at[stage, pl.ds(0, 3)],
+            dst_ref=grecv.at[stage, pl.ds(0, 3)],
+            send_sem=g_sem.at[2 + 2 * stage],
+            recv_sem=g_sem.at[3 + 2 * stage],
+            device_id={"ctx": ctx_peers[0]},
+            device_id_type=MESH,
+        )
+
+    gain_start(0)
     lax.fori_loop(0, CHUNKS, scan_backward, 0)
-
-    def gain_copy(p):
-        return pltpu.make_async_remote_copy(
-            src_ref=gboth,
-            dst_ref=grecv.at[me],
-            send_sem=g_sem.at[2],
-            recv_sem=g_sem.at[3],
-            device_id={"ctx": p},
-            device_id_type=MESH,
-        )
-
-    for p in ctx_peers:
-        gain_copy(p).start()
-    grecv[me] = gboth[...]
-    lax.fori_loop(HEADS_HERE // 4, HEADS_HERE, backward, 0)
+    gain_all(0).wait_recv()
+    gsum[1] = grecv[0, 0] + grecv[0, 1] + grecv[0, 2] + grecv[0, 3]
+    gain_start(1)
+    lax.fori_loop(3, HEADS_HERE, backward, 0)
 
     def sent(n, _):
         waiter(u.at[0], r1.at[0], send1.at[0], recv1.at[0], n).wait_send()
@@ -349,26 +366,16 @@
         for i in range(PER):
             h = n * PER + i
             recalled = state(1, n, i)
-            dk[:, lanes(h)] = (dki[h] + before[h] * dot(v[h], recalled, NT)).astype(BF16)
-            dv[:, lanes(h)] = (dvi[h] + before[h] * dot(k[h], recalled, NN)).astype(BF16)
+            dk[:, lanes(h)] = (dki[h] + before[h] * dot(v[h], recalled, NN)).astype(BF16)
+            dv[:, lanes(h)] = (dvi[h] + before[h] * dot(k[h], recalled, NT)).astype(BF16)
         return 0
 
     lax.fori_loop(0, CHUNKS, finish, 0)
 
-    gain_all = pltpu.make_async_remote_copy(
-        src_ref=grecv.at[pl.ds(0, CTX - 1)],
-        dst_ref=grecv.at[pl.ds(0, CTX - 1)],
-        send_sem=g_sem.at[2],
-        recv_sem=g_sem.at[3],
-        device_id={"ctx": ctx_peers[0]},
-        device_id_type=MESH,
-    )
-    gain_all.wait_recv()
-    gain_all.wait_send()
-    total = grecv[0]
-    for i in range(1, CTX):
-        total = total + grecv[i]
-    gain_out[...] = total
+    gain_all(1).wait_recv()
+    gain_out[...] = grecv[1, 0] + grecv[1, 1] + grecv[1, 2] + grecv[1, 3]
+    gain_all(0).wait_send()
+    gain_all(1).wait_send()
 
     def drain(n, _):
         waiter(s2.at[1], r2.at[1], send2.at[1], recv2.at[1], n).wait_send()
@@ -416,6 +423,7 @@
             heads32_t,
             heads32,
             heads32,
+            heads16,
             heads16_t,
             heads16_t,
             heads16,
@@ -435,13 +443,13 @@
             pltpu.VMEM((TP, 8, HD), F32),
             tile,
             tile,
-            tile,
-            pltpu.VMEM((CTX, HEADS_HERE, HD), F32),
+            pltpu.VMEM((2, HEADS_HERE, HD), F32),
+            pltpu.VMEM((2, 4, HEADS_HERE, HD), F32),
             dma((2,)),
             dma((5, HEADS_HERE)),
         ]
         + [dma((2, CHUNKS))] * 4
-        + [dma((TP - 1,)), dma((TP - 1,)), dma((4,))]
+        + [dma((TP - 1,)), dma((TP - 1,)), dma((6,))]
     )
     anywhere = pl.BlockSpec(memory_space=pl.ANY)
     in_hbm = pl.BlockSpec(memory_space=pltpu.HBM)

time: 46.6 us -> 45.9 us (0.985)
  Pallas kernels: 45.8 us -> 45.2 us
    pallas_call x1, Pallas kernels: 43.2 us -> 42.6 us  [per_device(): pl.pallas_call(kernel, out_shape=(flat, flat, flat, flat, tile), in_specs...]
where the time goes in v3:
time: 45.9 us
  Pallas kernels  45.2 us (98%)
  between operations  0.64 us (1%)
    pallas_call x1, Pallas kernels, per_device(): pl.pallas_call(kernel, out_shape=(flat, flat, flat, flat, tile), in_specs...  42.6 us
    pallas_call x1, Pallas kernels, per_device(): pl.pallas_call(place, out_shape=(whole, whole, whole, whole, jax.ShapeDty...  2.63 us

profile of v3, /device:TPU:2, one launch (start us, length us, event | category | flops | bytes accessed | tf_op | source)
XLA Modules:
  0.0 45.9 jit_solution(15439481374147518454)
XLA Ops:
  0.6 42.6 %lightning_backward.1 = (bf16[512,1024]{1,0:T(8,128)(2,1)S(1)}, bf16[512,1024]{1,0:T(8,128)(2,1)S(1)}, bf16[512,1024]{1,0:T(8,128)(2,1)S(1)}, bf16[512,1024]{1,0:T(8,128)(2,1)S(1)}, f32[8,128]{1,0:T(8,128)S(1)}) custom-call(f32[8]{0:T(128)} %slopes_in.1, bf16[1,512,1024]{2,1,0:T(8,128)(2,1)} %q_in.1, bf16[1,512,1024]{2,1,0:T(8,128)(2,1)} %k_in.1, ...), custom_call_target="tpu_custom_call" | custom-call | flops 3221225472 | bytes 5242880 | tf_op jit(solution)/shard_map/lightning_backward/pallas_call | solution.py:464
  43.2 2.6 %place_results.1 = (bf16[1,512,1024]{2,1,0:T(8,128)(2,1)}, bf16[1,512,1024]{2,1,0:T(8,128)(2,1)}, bf16[1,512,1024]{2,1,0:T(8,128)(2,1)}, bf16[1,512,1024]{2,1,0:T(8,128)(2,1)}, f32[8,128]{1,0:T(8,128)}) custom-call(bf16[512,1024]{1,0:T(8,128)(2,1)S(1)} %get-tuple-element.15.dq_in, bf16[512,1024]{1,0:T(8,128)(2,1)S(1)} %get-tuple-element.16.dk_in, ...), custom_call_target="tpu_custom_call" | custom-call | bytes 8388608 | tf_op jit(solution)/shard_map/place_results/pallas_call | solution.py:479

commit v4 on v3

--- a/solution.py
+++ b/solution.py
@@ -384,7 +384,7 @@
     lax.fori_loop(0, CHUNKS, drain, 0)
 
 
-def place(dq_in, dk_in, dv_in, dg_in, gain_in, dq, dk, dv, dg, gain, sem):
+def place(dq_in, dk_in, dv_in, dg_in, gain_in, dq, dk, dv, dg, gain, sem, gain_sem):
     pairs = ((dq_in, dq), (dk_in, dk), (dv_in, dv), (dg_in, dg))
     copies = [
         pltpu.make_async_copy(
@@ -393,9 +393,9 @@
         for i in range(BLOCK // PIECE)
         for n, (src, dst) in enumerate(pairs)
     ]
+    copies.append(pltpu.make_async_copy(gain_in, gain, gain_sem))
     for copy in copies:
         copy.start()
-    gain[...] = gain_in[...]
     for copy in copies:
         copy.wait()
 
@@ -480,8 +480,8 @@
         place,
         out_shape=(whole, whole, whole, whole, jax.ShapeDtypeStruct((HEADS_HERE, HD), F32)),
         in_specs=[in_vmem] * 5,
-        out_specs=(anywhere,) * 4 + (in_vmem,),
-        scratch_shapes=[dma((4, BLOCK // PIECE))],
+        out_specs=(anywhere,) * 5,
+        scratch_shapes=[dma((4, BLOCK // PIECE)), dma],
         compiler_params=pltpu.CompilerParams(vmem_limit_bytes=2 << 20),
         cost_estimate=pl.CostEstimate(flops=0, bytes_accessed=8 << 20, transcendentals=0),
         name="place_results",

time: 45.9 us -> 45.4 us (0.989)
  Pallas kernels: 45.2 us -> 44.6 us
    pallas_call x1, Pallas kernels: 2.63 us -> 2.05 us  [per_device(): pl.pallas_call(place, out_shape=(whole, whole, whole, whole, jax.ShapeDty...]
where the time goes in v4:
time: 45.4 us; the launch traced here: 45.3 us
  Pallas kernels  44.6 us (98%)
  between operations  0.64 us (1%)
    pallas_call x1, Pallas kernels, per_device(): pl.pallas_call(kernel, out_shape=(flat, flat, flat, flat, tile), in_specs...  42.6 us
    pallas_call x1, Pallas kernels, per_device(): pl.pallas_call(place, out_shape=(whole, whole, whole, whole, jax.ShapeDty...  2.05 us

profile of v4, /device:TPU:2, one launch (start us, length us, event | category | flops | bytes accessed | tf_op | source)
XLA Modules:
  0.0 45.3 jit_solution(8079476350912631053)
XLA Ops:
  0.6 42.6 %lightning_backward.1 = (bf16[512,1024]{1,0:T(8,128)(2,1)S(1)}, bf16[512,1024]{1,0:T(8,128)(2,1)S(1)}, bf16[512,1024]{1,0:T(8,128)(2,1)S(1)}, bf16[512,1024]{1,0:T(8,128)(2,1)S(1)}, f32[8,128]{1,0:T(8,128)S(1)}) custom-call(f32[8]{0:T(128)} %slopes_in.1, bf16[1,512,1024]{2,1,0:T(8,128)(2,1)} %q_in.1, bf16[1,512,1024]{2,1,0:T(8,128)(2,1)} %k_in.1, ...), custom_call_target="tpu_custom_call" | custom-call | flops 3221225472 | bytes 5242880 | tf_op jit(solution)/shard_map/lightning_backward/pallas_call | solution.py:464
  43.2 2.1 %place_results.1 = (bf16[1,512,1024]{2,1,0:T(8,128)(2,1)}, bf16[1,512,1024]{2,1,0:T(8,128)(2,1)}, bf16[1,512,1024]{2,1,0:T(8,128)(2,1)}, bf16[1,512,1024]{2,1,0:T(8,128)(2,1)}, f32[8,128]{1,0:T(8,128)}) custom-call(bf16[512,1024]{1,0:T(8,128)(2,1)S(1)} %get-tuple-element.15.dq_in, bf16[512,1024]{1,0:T(8,128)(2,1)S(1)} %get-tuple-element.16.dk_in, ...), custom_call_target="tpu_custom_call" | custom-call | bytes 8388608 | tf_op jit(solution)/shard_map/place_results/pallas_call | solution.py:479

commit v5 on v4

--- a/solution.py
+++ b/solution.py
@@ -313,7 +313,7 @@
         scan(1, n, True)
         return 0
 
-    lax.fori_loop(0, 3, backward, 0)
+    lax.fori_loop(0, 4, backward, 0)
     pair.wait_recv()
     gsum[0] = gsend[...] + gpart[...]
 
@@ -348,7 +348,7 @@
     gain_all(0).wait_recv()
     gsum[1] = grecv[0, 0] + grecv[0, 1] + grecv[0, 2] + grecv[0, 3]
     gain_start(1)
-    lax.fori_loop(3, HEADS_HERE, backward, 0)
+    lax.fori_loop(4, HEADS_HERE, backward, 0)
 
     def sent(n, _):
         waiter(u.at[0], r1.at[0], send1.at[0], recv1.at[0], n).wait_send()

time: 45.4 us -> 45.4 us (level)
  no operation moved by 1% of the time
where the time goes in v5:
time: 45.4 us; the launch traced here: 45.3 us
  Pallas kernels  44.6 us (98%)
  between operations  0.64 us (1%)
    pallas_call x1, Pallas kernels, per_device(): pl.pallas_call(kernel, out_shape=(flat, flat, flat, flat, tile), in_specs...  42.6 us
    pallas_call x1, Pallas kernels, per_device(): pl.pallas_call(place, out_shape=(whole, whole, whole, whole, jax.ShapeDty...  2.05 us

profile of v5, /device:TPU:2, one launch (start us, length us, event | category | flops | bytes accessed | tf_op | source)
XLA Modules:
  0.0 45.3 jit_solution(10897323073029845086)
XLA Ops:
  0.6 42.6 %lightning_backward.1 = (bf16[512,1024]{1,0:T(8,128)(2,1)S(1)}, bf16[512,1024]{1,0:T(8,128)(2,1)S(1)}, bf16[512,1024]{1,0:T(8,128)(2,1)S(1)}, bf16[512,1024]{1,0:T(8,128)(2,1)S(1)}, f32[8,128]{1,0:T(8,128)S(1)}) custom-call(f32[8]{0:T(128)} %slopes_in.1, bf16[1,512,1024]{2,1,0:T(8,128)(2,1)} %q_in.1, bf16[1,512,1024]{2,1,0:T(8,128)(2,1)} %k_in.1, ...), custom_call_target="tpu_custom_call" | custom-call | flops 3221225472 | bytes 5242880 | tf_op jit(solution)/shard_map/lightning_backward/pallas_call | solution.py:464
  43.2 2.1 %place_results.1 = (bf16[1,512,1024]{2,1,0:T(8,128)(2,1)}, bf16[1,512,1024]{2,1,0:T(8,128)(2,1)}, bf16[1,512,1024]{2,1,0:T(8,128)(2,1)}, bf16[1,512,1024]{2,1,0:T(8,128)(2,1)}, f32[8,128]{1,0:T(8,128)}) custom-call(bf16[512,1024]{1,0:T(8,128)(2,1)S(1)} %get-tuple-element.15.dq_in, bf16[512,1024]{1,0:T(8,128)(2,1)S(1)} %get-tuple-element.16.dk_in, ...), custom_call_target="tpu_custom_call" | custom-call | bytes 8388608 | tf_op jit(solution)/shard_map/place_results/pallas_call | solution.py:479
